TPU v7x, 512 devices: a whole 4x4x16 slice. The times are simulated.
512 devices in a mesh: patch: 64 (over z, y_hi, core), head: 8 (over x, y_lo).
Axes of the slice: x: 4, y: 4 (y_hi: 2, y_lo: 2; y = y_hi * 2 + y_lo), z: 16, core: 2. Of those that a mesh axis runs over, the one named last changes fastest.
Arguments:
- hidden_states: bfloat16 [8192, 3072], P('patch', 'head'), may hold values from -500 to 500, as said below
- shift_mod: float32 [3072], replicated, may hold values from -3 to 3
- scale_mod: float32 [3072], replicated, may hold values from -3 to 3
- gate_mod: float32 [3072], P('head'), may hold values from 1 to 6
- qkv_weight: bfloat16 [3072, 3, 2048], P('patch', None, 'head'), may hold values from -0.109375 to 0.109375
- query_gain: float32 [128], replicated, may hold values from 1 to 2.5
- key_gain: float32 [128], replicated, may hold values from 1 to 2.5
- text_keys: bfloat16 [512, 2048], P(None, 'head'), may hold values from -6 to 6
- text_values: bfloat16 [512, 2048], P(None, 'head'), may hold values from -6 to 6
- stale_keys: bfloat16 [8192, 2048], P('patch', 'head'), may hold values from -330 to 330, as said below
- stale_values: bfloat16 [8192, 2048], P('patch', 'head'), may hold values from -6 to 6
- out_weight: bfloat16 [2048, 3072], P('head'), may hold values from -0.125 to 0.125
Outputs:
- update: bfloat16 [8192, 3072], P('patch', 'head')
Inputs may be any that keep to these rules, and one draw needn't show every extreme that they name: `hidden_states`: finite real values. `stale_keys`: finite real values.
All inputs are finite; a program needn't handle non-finite values.
Results may differ from a plain program's by a relative error of at most 0.02.
The roundings to bfloat16 on the way count: a program that leaves them out, or rounds other values in their place, can miss the bound.
Values may be sent and summed in bfloat16 or wider, within the bound.
A program may use at most 64 MiB of HBM per device.

v0:
```python
import jax
import jax.numpy as jnp
from jax import lax
from jax.sharding import PartitionSpec as P


def head_norm(raw, gain):
    power = jnp.mean(raw * raw, axis=-1, keepdims=True)
    return raw * lax.rsqrt(power + 1e-06) * gain


def per_device(
    hidden_states,
    shift_mod,
    scale_mod,
    gate_mod,
    qkv_weight,
    query_gain,
    key_gain,
    text_keys,
    text_values,
    stale_keys,
    stale_values,
    out_weight,
):
    tok_rows = hidden_states.shape[0]
    local_width = qkv_weight.shape[2]
    head_size = query_gain.shape[0]
    local_heads = local_width // head_size
    gathered = lax.all_gather(hidden_states, "head", axis=1, tiled=True)
    states = gathered.astype(jnp.float32)
    center = jnp.mean(states, axis=-1, keepdims=True)
    spread = jnp.mean((states - center) ** 2, axis=-1, keepdims=True)
    normed = (states - center) * lax.rsqrt(spread + 1e-06)
    modulated = ((1.0 + scale_mod) * normed + shift_mod).astype(jnp.bfloat16)
    piece = lax.all_gather(qkv_weight, "patch", axis=0, tiled=True)
    flat_piece = piece.reshape(piece.shape[0], 3 * local_width)
    projected = jnp.dot(modulated, flat_piece, preferred_element_type=jnp.float32)
    projected = projected.reshape(tok_rows, 3, local_heads, head_size)
    queries = head_norm(projected[:, 0], query_gain).astype(jnp.bfloat16)
    fresh_keys = (
        head_norm(projected[:, 1], key_gain).astype(jnp.bfloat16).reshape(tok_rows, local_width)
    )
    fresh_values = projected[:, 2].astype(jnp.bfloat16).reshape(tok_rows, local_width)
    factor = head_size ** (-0.5)

    def scores_of(key_rows):
        shaped = key_rows.reshape(key_rows.shape[0], local_heads, head_size)
        return (
            jnp.einsum("qhd,khd->hqk", queries, shaped, preferred_element_type=jnp.float32) * factor
        )

    def values_of(exps, value_rows):
        shaped = value_rows.reshape(value_rows.shape[0], local_heads, head_size)
        return jnp.einsum(
            "hqk,khd->qhd", exps.astype(jnp.bfloat16), shaped, preferred_element_type=jnp.float32
        )

    first_keys = jnp.concatenate([text_keys, fresh_keys], axis=0)
    first_values = jnp.concatenate([text_values, fresh_values], axis=0)
    first_scores = scores_of(first_keys)
    running_max = jnp.max(first_scores, axis=-1)
    first_exps = jnp.exp(first_scores - running_max[:, :, None])
    running_totals = jnp.sum(first_exps, axis=-1)
    running_mixed = values_of(first_exps, first_values)
    own_start = lax.axis_index("patch") * tok_rows
    piece_keys = lax.all_gather(stale_keys, "patch", axis=0, tiled=True)
    piece_values = lax.all_gather(stale_values, "patch", axis=0, tiled=True)
    piece_rows = piece_keys.shape[0]
    scores = scores_of(piece_keys)
    positions = jnp.arange(piece_rows, dtype=jnp.int32)
    own_rows = (positions >= own_start) & (positions < own_start + tok_rows)
    scores = jnp.where(own_rows[None, None, :], -jnp.inf, scores)
    new_max = jnp.maximum(running_max, jnp.max(scores, axis=-1))
    rescale = jnp.exp(running_max - new_max)
    exps = jnp.exp(scores - new_max[:, :, None])
    new_totals = running_totals * rescale + jnp.sum(exps, axis=-1)
    new_mixed = running_mixed * jnp.transpose(rescale)[:, :, None] + values_of(exps, piece_values)
    attention = (
        (new_mixed / jnp.transpose(new_totals)[:, :, None])
        .astype(jnp.bfloat16)
        .reshape(tok_rows, local_width)
    )
    partial_terms = jnp.dot(attention, out_weight, preferred_element_type=jnp.float32)
    summed = lax.psum_scatter(
        partial_terms.astype(jnp.bfloat16), "head", scatter_dimension=1, tiled=True
    ).astype(jnp.float32)
    return (summed * gate_mod).astype(jnp.bfloat16)


def solution(mesh):
    placed = (
        P("patch", "head"),
        P(),
        P(),
        P("head"),
        P("patch", None, "head"),
        P(),
        P(),
        P(None, "head"),
        P(None, "head"),
        P("patch", "head"),
        P("patch", "head"),
        P("head", None),
    )
    return jax.shard_map(
        per_device, mesh=mesh, in_specs=placed, out_specs=P("patch", "head"), check_vma=False
    )
```

profile of v0, /device:TPU:1, one launch (start us, length us, event | category | flops | bytes accessed | tf_op | source)
XLA Modules:
  0.0 517.0 jit_solution(10268833403718431133)
XLA Ops:
  6.5 0.0 copy-start
  6.5 0.0 copy-start.2
  6.5 0.0 all-gather.8.cloned.1.call-start
  6.5 0.7 all-gather.8.cloned.1.call-update
  7.3 0.0 all-gather.4.cloned.1.call-start
  7.3 0.7 all-gather.4.cloned.1.call-update
  8.0 0.0 all-gather.6.cloned.1.call-start
  8.1 1.6 copy.29
  9.6 0.0 all-gather.6.cloned.1.call-update
  9.7 0.0 reduce-scatter.4.cloned.1.call-start
  9.7 1.1 copy.27
  10.8 0.2 copy.28
  11.0 1.1 copy.24
  12.1 25.2 %all_gather.12 = bf16[128,3072]{1,0:T(8,128)(2,1)S(1)} all-gather(bf16[128,384]{1,0:T(8,128)(2,1)} %param.12), channel_id=1, replica_groups=mesh['patch'=64,'head'=8] {'head'}, dimensions={1}, use_global_device_ids=true | all-gather | bytes 884736 | tf_op jit(solution)/shard_map/all_gather | solution.py:30
  37.3 0.2 convert_reduce_fusion
  37.5 0.4 fusion.8
  37.9 0.0 copy-done.2
  37.9 129.6 %all-gather.8.cloned.1.call-done = bf16[8192,256]{1,0:T(8,128)(2,1)} async-done(((bf16[128,256]{1,0:T(8,128)(2,1)}), bf16[8192,256]{1,0:T(8,128)(2,1)}) %all-gather.8.cloned.1.call-update) | async-done | bytes 4194320 | tf_op jit(solution)/shard_map/all_gather | solution.py:68
  167.5 6.4 %copy.31 = bf16[8192,256]{0,1:T(8,128)(2,1)} copy(bf16[8192,256]{1,0:T(8,128)(2,1)} %all-gather.8.cloned.1.call-done) | data formatting | bytes 8388608 | tf_op jit(solution)/shard_map/all_gather | solution.py:68
  173.9 0.0 copy-start.6
  173.9 144.6 %all-gather.4.cloned.1.call-done = bf16[3072,3,256]{2,0,1:T(8,128)(2,1)} async-done(((bf16[48,3,256]{2,0,1:T(8,128)(2,1)}), bf16[3072,3,256]{2,0,1:T(8,128)(2,1)}) %all-gather.4.cloned.1.call-update) | async-done | bytes 4718608 | tf_op jit(solution)/shard_map/all_gather | solution.py:36
  318.5 6.7 %copy.25 = bf16[3072,3,256]{0,2,1:T(8,128)(2,1)} copy(bf16[3072,3,256]{2,0,1:T(8,128)(2,1)} %all-gather.4.cloned.1.call-done) | data formatting | bytes 9437184 | tf_op jit(solution)/shard_map/all_gather | solution.py:36
  325.2 0.0 copy-start.5
  325.2 0.0 copy-start.3
  325.2 0.0 copy-done.6
  325.2 4.1 fusion.20
  329.2 0.1 multiply_reduce_fusion
  329.4 0.0 copy-done.5
  329.4 0.1 multiply_convert_fusion.1
  329.5 134.3 %all-gather.6.cloned.1.call-done = bf16[8192,256]{0,1:T(8,128)(2,1)} async-done(((bf16[128,256]{0,1:T(8,128)(2,1)}), bf16[8192,256]{0,1:T(8,128)(2,1)}) %all-gather.6.cloned.1.call-update) | async-done | bytes 4194320 | tf_op jit(solution)/shard_map/all_gather | solution.py:67
  463.8 0.0 copy-done.3
  463.8 3.9 fusion.43
  467.7 0.4 fusion.42
  468.1 0.0 copy-start.1
  468.1 1.3 fusion.1
  469.4 0.9 copy-done.1
  470.3 1.3 fusion.15
  471.6 0.0 copy-start.4
  471.6 0.1 copy.26
  471.8 0.2 fusion.26
  472.0 0.4 fusion.18
  472.4 0.0 copy-done
  472.4 0.4 convolution_convert_fusion
  472.8 1.2 copy.34
  474.0 0.0 reduce-scatter.4.cloned.1.call-update
  474.0 34.8 %reduce-scatter.4.cloned.1.call-done = bf16[384,128]{1,0:T(8,128)(2,1)} async-done(((bf16[3072,128]{1,0:T(8,128)(2,1)}), bf16[384,128]{1,0:T(8,128)(2,1)}) %reduce-scatter.4.cloned.1.call-update) | async-done | bytes 98320
  508.8 1.0 copy.35
  509.8 0.0 copy-done.4
  509.8 0.7 multiply_convert_fusion
  (9 shorter events, 0.1 us)
Async XLA Ops:
  6.5 465.9 %copy-start = (bf16[256,3072]{1,0:T(8,128)(2,1)S(1)}, bf16[256,3072]{1,0:T(8,128)(2,1)}, u32[]{:S(2)}) copy-start(bf16[256,3072]{1,0:T(8,128)(2,1)} %param.23) | copy-start | bytes 4718596
  6.5 31.3 %copy-start.2 = (f32[3072]{0:T(1024)S(1)}, f32[3072]{0:T(1024)}, u32[]{:S(2)}) copy-start(f32[3072]{0:T(1024)} %param.14) | copy-start | bytes 36868
  6.5 160.9 %all-gather.8.cloned.1.call-start = ((), (), s32[]{:S(2)}) async-start(), calls=%async_computation.3 | async-start | bytes 4259840 | tf_op jit(solution)/shard_map/all_gather | solution.py:68
  7.3 311.2 %all-gather.4.cloned.1.call-start = ((), (), s32[]{:S(2)}) async-start(), calls=%async_computation.1 | async-start | bytes 4792320 | tf_op jit(solution)/shard_map/all_gather | solution.py:36
  8.0 455.8 %all-gather.6.cloned.1.call-start = ((), (), s32[]{:S(2)}) async-start(), calls=%async_computation.2 | async-start | bytes 4259840 | tf_op jit(solution)/shard_map/all_gather | solution.py:67
  9.7 499.1 %reduce-scatter.4.cloned.1.call-start = ((), (), s32[]{:S(2)}) async-start(), calls=%async_computation.4 | async-start | bytes 884736
  173.9 151.3 %copy-start.6 = (f32[3072]{0:T(1024)S(1)}, f32[3072]{0:T(1024)}, u32[]{:S(2)}) copy-start(f32[3072]{0:T(1024)} %param.13) | copy-start | bytes 36868
  325.2 4.3 copy-start.5
  325.2 138.7 %copy-start.3 = (f32[128]{0:T(128)S(1)}, f32[128]{0:T(128)}, u32[]{:S(2)}) copy-start(f32[128]{0:T(128)} %param.17) | copy-start | bytes 1540
  468.1 2.2 copy-start.1
  471.6 38.2 %copy-start.4 = (f32[384]{0:T(512)S(1)}, f32[384]{0:T(512)}, u32[]{:S(2)}) copy-start(f32[384]{0:T(512)} %param.15) | copy-start | bytes 4612
Sparse Core Ops, SparseCore 0:
  10.7 156.7 all-gather.7
  170.7 147.7 all-gather.3
  321.5 142.3 all-gather.5
  474.1 34.6 reduce-scatter.3
where the time goes:
time: 521 us; the launch traced here: 517 us
  waiting for transfers between devices  445 us (85%)
  blocking collectives  25.2 us (5%)
  local copies, waits for them, and re-layouts  20.2 us (4%)
  between operations  13.3 us (3%)
  matrix products  10.4 us (2%)
    all_gather x1, waiting for transfers between devices, per_device(): piece = lax.all_gather(qkv_weight, 'patch', axis=0, tiled=True)  145 us
    all_gather x1, waiting for transfers between devices, per_device(): piece_keys = lax.all_gather(stale_keys, 'patch', axis=0, tiled=True)  134 us
    all_gather x1, waiting for transfers between devices, per_device(): piece_values = lax.all_gather(stale_values, 'patch', axis=0, tiled=True)  130 us
    unnamed x5, waiting for transfers between devices  36.2 us
    all_gather x1, blocking collectives, per_device(): gathered = lax.all_gather(hidden_states, 'head', axis=1, tiled=True)  25.2 us
  transfers between devices with their start and end apart: 4, of which 4 were waited for; matrix products, arithmetic and copies ran while one was open for 4% of the time, Pallas kernels for 0%

commit v1 on v0

v1 whole, which is shorter than its diff:
```python
import functools
import math

import jax
import jax.numpy as jnp
from jax import lax
from jax.experimental import pallas as pl
from jax.experimental.pallas import tpu as pltpu
from jax.sharding import PartitionSpec as P

MESH = pl.DeviceIdType.MESH
NZ = 16
F32 = jnp.float32
BF16 = jnp.bfloat16
COPY = pltpu.make_async_remote_copy
EXP_SCALE = 128 ** (-0.5) * math.log2(math.e)
PEERS = [(dx, dl, dh) for dh in (0, 1) for dl in (0, 1) for dx in range(4)][1:]
OUT_PEERS = [(dx, dl) for dl in (0, 1) for dx in range(4)][1:]


def kernel(
    hidden,
    shift,
    scale,
    gate,
    weight,
    query_gain,
    key_gain,
    text_keys,
    text_values,
    stale_keys,
    stale_values,
    out_weight,
    out,
    hid,
    mod,
    wbuf,
    kv,
    text,
    wo,
    gathered,
    mine,
    own,
    proj,
    queries,
    peak,
    total,
    mixed,
    loc_sem,
    swap_send,
    swap_recv,
    ring_send,
    ring_recv,
    sib_send,
    sib_recv,
    hid_send,
    hid_recv,
    wo_send,
    wo_recv,
    wos_send,
    wos_recv,
    att_send,
    att_recv,
):
    me = lax.axis_index("patch")
    group = lax.axis_index("head")
    z, yh, c = me // 4, lax.rem(me // 2, 2), lax.rem(me, 2)
    x, yl = group // 2, lax.rem(group, 2)
    head = group * 2 + yh
    other_core = (z * 4 + yh * 2 + 1 - c, group)
    next_z = (lax.rem(z + 1, NZ) * 4 + yh * 2 + c, group)
    last_z = (lax.rem(z + NZ - 1, NZ) * 4 + yh * 2 + c, group)
    swap = (z * 4 + (1 - yh) * 2 + c, group)

    def plane_peer(dx, dl, dh):
        there = lax.rem(x + dx, 4) * 2 + lax.rem(yl + dl, 2)
        return (z * 4 + lax.rem(yh + dh, 2) * 2 + c, there)

    barrier = pltpu.get_barrier_semaphore()
    everyone = [other_core, next_z, last_z] + [plane_peer(*d) for d in PEERS]
    for peer in everyone:
        pl.semaphore_signal(barrier, inc=1, device_id=peer, device_id_type=MESH)

    here = pl.ds(pl.multiple_of(yh * 128, 128), 128)
    there = pl.ds(pl.multiple_of((1 - yh) * 128, 128), 128)
    columns = pl.ds(pl.multiple_of(group * 384, 384), 384)
    local = [
        pltpu.make_async_copy(weight.at[yh], wbuf.at[me], loc_sem.at[0]),
        pltpu.make_async_copy(stale_keys.at[:, here], kv.at[me, pl.ds(0, 128)], loc_sem.at[1]),
        pltpu.make_async_copy(stale_values.at[:, here], kv.at[me, pl.ds(128, 128)], loc_sem.at[2]),
        pltpu.make_async_copy(hidden, hid.at[yh, group], loc_sem.at[3]),
        pltpu.make_async_copy(text_keys.at[:, here], text.at[0], loc_sem.at[4]),
        pltpu.make_async_copy(text_values.at[:, here], text.at[1], loc_sem.at[5]),
        pltpu.make_async_copy(out_weight.at[:, columns], wo.at[group], loc_sem.at[6]),
    ]
    for copy in local:
        copy.start()

    pl.semaphore_wait(barrier, len(everyone))

    def chunk(kind, stream, offset, core):
        side = yh if stream == 0 else 1 - yh
        index = lax.rem(z + offset + NZ, NZ) * 4 + side * 2 + core
        return (wbuf if kind == 0 else kv).at[index]

    def ring(kind, stream, way, step):
        ref = chunk(kind, stream, (1 - step) if way == 0 else (step - 1), c)
        at = (kind * 2 + stream) * 2 + way
        return COPY(
            ref, ref, ring_send.at[at, step], ring_recv.at[at, step],
            device_id=next_z if way == 0 else last_z, device_id_type=MESH,
        )

    def ring_arrival(kind, stream, way, step):
        ref = chunk(kind, stream, -step if way == 0 else step, c)
        at = (kind * 2 + stream) * 2 + way
        return COPY(
            ref, ref, ring_send.at[at, step], ring_recv.at[at, step],
            device_id=next_z if way == 0 else last_z, device_id_type=MESH,
        )

    def sibling(kind, stream, offset, core):
        ref = chunk(kind, stream, offset, core)
        at, slot = kind * 2 + stream, lax.rem(offset + NZ, NZ)
        return COPY(
            ref, ref, sib_send.at[at, slot], sib_recv.at[at, slot],
            device_id=other_core, device_id_type=MESH,
        )

    def swap_copy(src, dst, at):
        return COPY(
            src, dst, swap_send.at[at], swap_recv.at[at], device_id=swap, device_id_type=MESH
        )

    swaps = [
        swap_copy(weight.at[1 - yh], wbuf.at[me], 0),
        swap_copy(stale_keys.at[:, there], kv.at[me, pl.ds(0, 128)], 1),
        swap_copy(stale_values.at[:, there], kv.at[me, pl.ds(128, 128)], 2),
    ]
    partner = z * 4 + (1 - yh) * 2 + c
    swap_arrivals = [
        swap_copy(weight.at[1 - yh], wbuf.at[partner], 0),
        swap_copy(stale_keys.at[:, there], kv.at[partner, pl.ds(0, 128)], 1),
        swap_copy(stale_values.at[:, there], kv.at[partner, pl.ds(128, 128)], 2),
    ]

    def hid_copy(at, dx, dl, dh):
        return COPY(
            hidden, hid.at[yh, group], hid_send.at[at], hid_recv.at[at],
            device_id=plane_peer(dx, dl, dh), device_id_type=MESH,
        )

    def source_group(dx, dl):
        return lax.rem(x + 4 - dx, 4) * 2 + lax.rem(yl + dl, 2)

    def hid_arrival(at, dx, dl, dh):
        slot = hid.at[lax.rem(yh + dh, 2), source_group(dx, dl)]
        return COPY(
            slot, slot, hid_send.at[at], hid_recv.at[at],
            device_id=plane_peer(dx, dl, dh), device_id_type=MESH,
        )

    half = pl.ds(pl.multiple_of(c * 128, 128), 128)
    other_half = pl.ds(pl.multiple_of((1 - c) * 128, 128), 128)

    def wo_copy(at, dx, dl):
        peer = plane_peer(dx, dl, 0)
        src = out_weight.at[half, pl.ds(pl.multiple_of(peer[1] * 384, 384), 384)]
        return COPY(
            src, wo.at[group, half], wo_send.at[at], wo_recv.at[at],
            device_id=peer, device_id_type=MESH,
        )

    def wo_arrival(at, dx, dl):
        slot = wo.at[source_group(dx, dl), half]
        return COPY(
            slot, slot, wo_send.at[at], wo_recv.at[at],
            device_id=plane_peer(dx, dl, 0), device_id_type=MESH,
        )

    def wo_share(at, dx, dl, rows):
        slot = wo.at[source_group(dx, dl), rows]
        return COPY(
            slot, slot, wos_send.at[at], wos_recv.at[at],
            device_id=other_core, device_id_type=MESH,
        )

    swaps[0].start()
    local[0].wait()
    ring(0, 0, 0, 1).start()
    ring(0, 0, 1, 1).start()
    swaps[1].start()
    swaps[2].start()
    sibling(0, 0, 0, c).start()
    local[1].wait()
    local[2].wait()
    ring(1, 0, 0, 1).start()
    ring(1, 0, 1, 1).start()
    sibling(1, 0, 0, c).start()
    for at, d in enumerate(PEERS):
        hid_copy(at, *d).start()
    swap_arrivals[0].wait_recv()
    ring(0, 1, 0, 1).start()
    ring(0, 1, 1, 1).start()
    sibling(0, 1, 0, c).start()
    swap_arrivals[1].wait_recv()
    swap_arrivals[2].wait_recv()
    ring(1, 1, 0, 1).start()
    ring(1, 1, 1, 1).start()
    sibling(1, 1, 0, c).start()
    for at, d in enumerate(OUT_PEERS):
        wo_copy(at, *d).start()

    def forward(kind, step):
        for stream in (0, 1):
            for way in (0, 1):
                ring_arrival(kind, stream, way, step).wait_recv()
                ring(kind, stream, way, step + 1).start()
                sibling(kind, stream, -step if way == 0 else step, c).start()

    def forward_seventh(kind):
        for stream in (0, 1):
            for way in (0, 1):
                ring_arrival(kind, stream, way, 7).wait_recv()
                if stream == way:
                    ring(kind, stream, way, 8).start()
                sibling(kind, stream, -7 if way == 0 else 7, c).start()

    def forward_eighth(kind):
        for way in (0, 1):
            ring_arrival(kind, way, way, 8).wait_recv()
            sibling(kind, way, 8, c).start()

    @pl.loop(1, 7)
    def _(step):
        forward(0, step)

    forward_seventh(0)
    forward(1, 1)
    forward_eighth(0)
    forward(1, 2)

    def norm(side):
        @pl.loop(0, 8)
        def _(block):
            rows = pl.ds(pl.multiple_of(block * 16, 16), 16)
            states = jnp.concatenate([hid[side, g, rows, :] for g in range(8)], axis=1)
            states = states.astype(F32)
            center = jnp.mean(states, axis=-1, keepdims=True)
            states = states - center
            spread = jnp.mean(states * states, axis=-1, keepdims=True)
            normed = states * lax.rsqrt(spread + 1e-06)
            modulated = (1.0 + scale[...]) * normed + shift[...]
            there = pl.ds(pl.multiple_of(side * 128 + block * 16, 16), 16)
            mod[there, :] = modulated.astype(BF16)

    local[3].wait()
    for at, d in enumerate(PEERS):
        hid_arrival(at, *d).wait_recv()
    norm(0)
    forward(1, 3)
    norm(1)

    @pl.loop(0, NZ)
    def _(slot):
        sibling(0, 0, slot, 1 - c).wait_recv()
        sibling(0, 1, slot, 1 - c).wait_recv()

    proj[...] = jnp.zeros_like(proj)

    @pl.loop(0, 8)
    def _(part):
        features = pl.ds(pl.multiple_of(part * 384, 384), 384)
        rows = wbuf[pl.ds(part * 8, 8)].reshape(384, 384)
        proj[...] += jnp.dot(mod[:, features], rows, preferred_element_type=F32)

    forward(1, 4)

    def head_norm(raw, gain):
        power = jnp.mean(raw * raw, axis=-1, keepdims=True)
        return (raw * lax.rsqrt(power + 1e-06) * gain).astype(BF16)

    queries[...] = head_norm(proj[:, 0:128], query_gain[...])

    def scores_of(rows, keys):
        return lax.dot_general(
            queries[rows, :], keys, (((1,), (1,)), ((), ())), preferred_element_type=F32
        )

    def lane_sums(exps):
        parts = [exps[:, i : i + 128] for i in range(0, exps.shape[1], 128)]
        return functools.reduce(lambda a, b: a + b, parts)

    def start_attend(rows, keys, values):
        scores = scores_of(rows, keys)
        top = jnp.max(scores, axis=-1, keepdims=True)
        exps = jnp.exp2((scores - top) * EXP_SCALE)
        peak[rows, :] = jnp.broadcast_to(top, (scores.shape[0], 128))
        total[rows, :] = lane_sums(exps)
        mixed[rows, :] = jnp.dot(exps.astype(BF16), values, preferred_element_type=F32)

    def attend(rows, keys, values):
        scores = scores_of(rows, keys)
        before = peak[rows, :]
        top = jnp.maximum(before, jnp.max(scores, axis=-1, keepdims=True))
        rescale = jnp.exp2((before - top) * EXP_SCALE)
        exps = jnp.exp2((scores - top[:, 0:1]) * EXP_SCALE)
        peak[rows, :] = top
        total[rows, :] = total[rows, :] * rescale + lane_sums(exps)
        mixed[rows, :] = mixed[rows, :] * rescale + jnp.dot(
            exps.astype(BF16), values, preferred_element_type=F32
        )

    every = pl.ds(0, 256)
    local[4].wait()
    local[5].wait()
    start_attend(every, text[0], text[1])

    sibling(1, 0, 0, 1 - c).wait_recv()
    sibling(1, 1, 0, 1 - c).wait_recv()
    for side in (0, 1):
        rows = pl.ds(side * 128, 128)
        own[...] = kv[pl.ds(z * 4, 4)]
        own[side * 2 + c, 0:128, :] = head_norm(proj[rows, 128:256], key_gain[...])
        own[side * 2 + c, 128:256, :] = proj[rows, 256:384].astype(BF16)
        attend(rows, own[:, 0:128, :].reshape(512, 128), own[:, 128:256, :].reshape(512, 128))

    def attend_plane(offset):
        sibling(1, 0, offset, 1 - c).wait_recv()
        sibling(1, 1, offset, 1 - c).wait_recv()
        base = lax.rem(z + offset + NZ, NZ) * 4
        keys = kv[pl.ds(base, 4), 0:128, :].reshape(512, 128)
        values = kv[pl.ds(base, 4), 128:256, :].reshape(512, 128)
        attend(every, keys, values)

    def attend_pairs(first, count):
        @pl.loop(0, 2 * count)
        def _(i):
            distance = first + i // 2
            attend_plane(lax.rem(i, 2) * (NZ - 2 * distance) + distance)

    forward(1, 5)
    attend_pairs(1, 2)
    forward(1, 6)
    for at, d in enumerate(OUT_PEERS):
        wo_arrival(at, *d).wait_recv()
        wo_share(at, *d, half).start()
    attend_pairs(3, 2)
    forward_seventh(1)
    attend_pairs(5, 2)
    forward_eighth(1)
    attend_pairs(7, 1)
    attend_plane(8)

    attention = (mixed[...] / jnp.sum(total[...], axis=-1, keepdims=True)).astype(BF16)
    mine[0] = attention[0:128]
    mine[1] = attention[128:256]
    gathered[head] = mine[yh]

    def att_copy(at, dx, dl, dh):
        return COPY(
            mine.at[lax.rem(yh + dh, 2)], gathered.at[head], att_send.at[at], att_recv.at[at],
            device_id=plane_peer(dx, dl, dh), device_id_type=MESH,
        )

    def att_arrival(at, dx, dl, dh):
        slot = gathered.at[source_group(dx, dl) * 2 + lax.rem(yh + dh, 2)]
        return COPY(
            slot, slot, att_send.at[at], att_recv.at[at],
            device_id=plane_peer(dx, dl, dh), device_id_type=MESH,
        )

    for at, d in enumerate(PEERS):
        att_copy(at, *d).start()
    local[6].wait()
    for at, d in enumerate(OUT_PEERS):
        wo_share(at, *d, other_half).wait_recv()
    for at, d in enumerate(PEERS):
        att_arrival(at, *d).wait_recv()
    summed = jnp.zeros((128, 384), F32)
    for g in range(8):
        left = jnp.concatenate([gathered[2 * g], gathered[2 * g + 1]], axis=1)
        summed += jnp.dot(left, wo[g], preferred_element_type=F32)
    out[...] = (summed * gate[...]).astype(BF16)

    for copy in swaps:
        copy.wait_send()
    for at, d in enumerate(PEERS):
        hid_copy(at, *d).wait_send()
        att_copy(at, *d).wait_send()
    for at, d in enumerate(OUT_PEERS):
        wo_copy(at, *d).wait_send()
        wo_share(at, *d, half).wait_send()
    for kind in (0, 1):
        for stream in (0, 1):
            for way in (0, 1):
                @pl.loop(1, 8)
                def _(step):
                    ring(kind, stream, way, step).wait_send()
            ring(kind, stream, stream, 8).wait_send()

            @pl.loop(0, NZ)
            def _(slot):
                sibling(kind, stream, slot, c).wait_send()


def per_device(
    hidden_states,
    shift_mod,
    scale_mod,
    gate_mod,
    qkv_weight,
    query_gain,
    key_gain,
    text_keys,
    text_values,
    stale_keys,
    stale_values,
    out_weight,
):
    weight = qkv_weight.reshape(48, 3, 2, 128).transpose(2, 0, 1, 3).reshape(2, 48, 384)
    dma = pltpu.SemaphoreType.DMA
    vmem = pl.BlockSpec(memory_space=pltpu.VMEM)
    hbm = pl.BlockSpec(memory_space=pl.ANY)
    n, m = len(PEERS), len(OUT_PEERS)
    return pl.pallas_call(
        kernel,
        name="joint_attention",
        out_shape=jax.ShapeDtypeStruct((128, 384), BF16),
        in_specs=[hbm, vmem, vmem, vmem, hbm, vmem, vmem, hbm, hbm, hbm, hbm, hbm],
        out_specs=vmem,
        scratch_shapes=[
            pltpu.VMEM((2, 8, 128, 384), BF16),
            pltpu.VMEM((256, 3072), BF16),
            pltpu.VMEM((64, 48, 384), BF16),
            pltpu.VMEM((64, 256, 128), BF16),
            pltpu.VMEM((2, 512, 128), BF16),
            pltpu.VMEM((8, 256, 384), BF16),
            pltpu.VMEM((16, 128, 128), BF16),
            pltpu.VMEM((2, 128, 128), BF16),
            pltpu.VMEM((4, 256, 128), BF16),
            pltpu.VMEM((256, 384), F32),
            pltpu.VMEM((256, 128), BF16),
            pltpu.VMEM((256, 128), F32),
            pltpu.VMEM((256, 128), F32),
            pltpu.VMEM((256, 128), F32),
            dma((7,)),
            dma((3,)),
            dma((3,)),
            dma((8, 9)),
            dma((8, 9)),
            dma((4, NZ)),
            dma((4, NZ)),
            dma((n,)),
            dma((n,)),
            dma((m,)),
            dma((m,)),
            dma((m,)),
            dma((m,)),
            dma((n,)),
            dma((n,)),
        ],
        compiler_params=pltpu.CompilerParams(
            collective_id=0, has_side_effects=True, vmem_limit_bytes=48 * 1024 * 1024
        ),
        cost_estimate=pl.CostEstimate(
            flops=2_200_000_000, bytes_accessed=16_000_000, transcendentals=2_300_000
        ),
    )(
        hidden_states,
        shift_mod.reshape(1, -1),
        scale_mod.reshape(1, -1),
        gate_mod.reshape(1, -1),
        weight,
        query_gain.reshape(1, -1),
        key_gain.reshape(1, -1),
        text_keys,
        text_values,
        stale_keys,
        stale_values,
        out_weight,
    )


def solution(mesh):
    placed = (
        P("patch", "head"),
        P(),
        P(),
        P("head"),
        P("patch", None, "head"),
        P(),
        P(),
        P(None, "head"),
        P(None, "head"),
        P("patch", "head"),
        P("patch", "head"),
        P("head", None),
    )
    return jax.shard_map(
        per_device, mesh=mesh, in_specs=placed, out_specs=P("patch", "head"), check_vma=False
    )
```

time: 521 us -> 111 us (0.21)
  waiting for transfers between devices: 445 us -> 0 us
  Pallas kernels: 0 us -> 97.9 us
  blocking collectives: 25.2 us -> 0 us
  between operations: 13.3 us -> 0.04 us
  matrix products: 10.4 us -> 0 us
  local copies, waits for them, and re-layouts: 20.2 us -> 10.9 us
    all_gather x3 -> x0, waiting for transfers between devices: 408 us -> none  [the longest x1 145 us: per_device(): piece = lax.all_gather(qkv_weight, 'patch', axis=0, tiled=True)]
    pallas_call x0 -> x1, Pallas kernels: none -> 97.9 us  [per_device(): pl.pallas_call(kernel, name='joint_attention', out_shape=jax.ShapeDtypeSt...]
    unnamed x5 -> x0, waiting for transfers between devices: 36.2 us -> none
    all_gather x1 -> x0, blocking collectives: 25.2 us -> none  [per_device(): gathered = lax.all_gather(hidden_states, 'head', axis=1, tiled=True)]
    all_gather x2 -> x0, local copies, waits for them, and re-layouts: 13.1 us -> none  [the longest x1 6.71 us: per_device(): piece = lax.all_gather(qkv_weight, 'patch', axis=0, tiled=True)]
    dot_general x6 -> x0, matrix products: 10.4 us -> none  [the longest x2 4.26 us: scores_of(): jnp.einsum('qhd,khd->hqk', queries, shaped, preferred_element_type=jnp.fl...]
  transfers between devices with their start and end apart: 4 -> 0, of which waited for: 4 -> 0; matrix products, arithmetic and copies ran while one was open for 4% -> 0% of each run, Pallas kernels for 0% -> 0%
where the time goes in v1:
time: 111 us; the launch traced here: 109 us
  Pallas kernels  97.9 us (88%)
  local copies, waits for them, and re-layouts  10.9 us (10%)
    pallas_call x1, Pallas kernels, per_device(): pl.pallas_call(kernel, name='joint_attention', out_shape=jax.ShapeDtypeSt...  97.9 us
    unnamed x21, local copies, waits for them, and re-layouts  9.24 us

profile of v1, /device:TPU:1, one launch (start us, length us, event | category | flops | bytes accessed | tf_op | source)
XLA Modules:
  0.0 108.9 jit_solution(17402438012671962875)
XLA Ops:
  0.0 0.7 reshape.23.gate
  0.7 0.9 reshape.24
  1.6 0.1 copy.16
  1.6 0.1 reshape.25.weight
  1.7 0.0 copy-start
  1.7 1.4 %copy-done = bf16[256,3072]{1,0:T(8,128)(2,1)S(1)} copy-done((bf16[256,3072]{1,0:T(8,128)(2,1)S(1)}, bf16[256,3072]{1,0:T(8,128)(2,1)}, u32[]{:S(2)}) %copy-start) | copy-done | bytes 1572888
  3.1 0.0 copy-start.1
  3.1 0.9 copy-done.1
  4.1 0.0 copy-start.2
  4.1 0.9 copy-done.2
  5.0 0.0 copy-start.3
  5.0 0.9 copy-done.3
  5.9 0.0 copy-start.4
  5.9 0.8 copy-done.4
  6.8 0.0 copy-start.5
  6.8 0.8 copy-done.5
  7.6 0.0 copy-start.6
  7.6 0.7 copy-done.6
  8.3 0.0 copy-start.7
  8.3 0.7 copy-done.7
  9.0 0.0 copy-start.8
  9.0 0.7 copy-done.8
  9.7 0.0 copy-start.9
  9.7 0.7 copy-done.9
  10.3 97.9 %joint_attention.1 = bf16[128,384]{1,0:T(8,128)(2,1)S(1)} custom-call(bf16[128,384]{1,0:T(8,128)(2,1)S(1)} %copy-done.3, f32[1,3072]{1,0:T(1,128)S(1)} %bitcast.9, f32[1,3072]{1,0:T(1,128)S(1)} %bitcast.10, f32[1,384]{1,0:T(1,128)S(1)} %reshape.23.gate, bf16[2,48,384]{2,1,0:T(8,128)(2,1)S(1)} %reshape.25.weight, f32[1,128]{1,0:T(1,128)S(1)} %bitcast.11, ...), custom_call_target="tpu_custom_call" | custom-call | flops 2200000000 | bytes 16000000 | tf_op jit(solution)/shard_map/joint_attention/pallas_call | solution.py:426
  108.3 0.6 copy.18
Async XLA Ops:
  1.7 1.4 %copy-start = (bf16[256,3072]{1,0:T(8,128)(2,1)S(1)}, bf16[256,3072]{1,0:T(8,128)(2,1)}, u32[]{:S(2)}) copy-start(bf16[256,3072]{1,0:T(8,128)(2,1)} %out_weight.1) | copy-start | bytes 4718596
  3.1 0.9 copy-start.1
  4.1 0.9 copy-start.2
  5.0 0.9 copy-start.3
  5.9 0.8 copy-start.4
  6.8 0.8 copy-start.5
  7.6 0.7 copy-start.6
  8.3 0.7 copy-start.7
  9.0 0.7 copy-start.8
  9.7 0.7 copy-start.9

commit v2 on v1

v2 whole, which is shorter than its diff:
```python
import functools

import math

import jax
import jax.numpy as jnp
from jax import lax
from jax.experimental import pallas as pl
from jax.experimental.pallas import tpu as pltpu
from jax.sharding import PartitionSpec as P

MESH = pl.DeviceIdType.MESH
ORDER = (
    ("W", 0, 1), ("K", 0, 1), ("W", 1, 0), ("V", 0, 1), ("K", 1, 0), ("W", 0, 2), ("V", 1, 0), ("W", 1, 1),
    ("K", 0, 2), ("W", 0, 3), ("V", 0, 2), ("W", 1, 2), ("K", 1, 1), ("V", 1, 1), ("W", 0, 4), ("K", 0, 3),
    ("W", 1, 3), ("V", 0, 3), ("K", 1, 2), ("W", 0, 5), ("V", 1, 2), ("W", 1, 4), ("K", 0, 4), ("V", 0, 4),
    ("W", 0, 6), ("K", 1, 3), ("W", 1, 5), ("V", 1, 3), ("N", 0, 0), ("K", 0, 5), ("N", 1, 0), ("W", 0, 7),
    ("N", 2, 0), ("V", 0, 5), ("N", 3, 0), ("K", 1, 4), ("W", 1, 6), ("V", 1, 4), ("W", 0, 8), ("K", 0, 6),
    ("V", 0, 6), ("K", 1, 5), ("W", 1, 7), ("V", 1, 5), ("K", 0, 7), ("V", 0, 7), ("K", 1, 6), ("W", 1, 8),
    ("V", 1, 6), ("K", 0, 8), ("P", 0, 0), ("V", 0, 8), ("K", 1, 7), ("O", 0, 0), ("S", 0, 0), ("V", 1, 7),
    ("A", 1, 2), ("K", 1, 8), ("A", 3, 1), ("V", 1, 8), ("A", 4, 4), ("L", 0, 0),
)
WEIGHTS, KEYS, VALUES = "WKV"
KINDS = (WEIGHTS, KEYS, VALUES)

NZ = 16
F32 = jnp.float32
BF16 = jnp.bfloat16
COPY = pltpu.make_async_remote_copy
EXP_SCALE = 128 ** (-0.5) * math.log2(math.e)
PEERS = [(dx, dl, dh) for dh in (0, 1) for dl in (0, 1) for dx in range(4)][1:]
OUT_PEERS = [(dx, dl) for dl in (0, 1) for dx in range(4)][1:]


def kernel(
    hidden,
    shift,
    scale,
    gate,
    weight,
    query_gain,
    key_gain,
    text_keys,
    text_values,
    stale_keys,
    stale_values,
    out_weight,
    out,
    hid,
    mod,
    wbuf,
    kbuf,
    vbuf,
    shift_row,
    scale_row,
    gate_row,
    gains,
    text,
    wo,
    gathered,
    mine,
    own_keys,
    own_values,
    proj,
    queries,
    peak,
    total,
    mixed,
    loc_sem,
    swap_send,
    swap_recv,
    ring_send,
    ring_recv,
    sib_send,
    sib_recv,
    hid_send,
    hid_recv,
    wo_send,
    wo_recv,
    wos_send,
    wos_recv,
    att_send,
    att_recv,
):
    me = lax.axis_index("patch")
    group = lax.axis_index("head")
    z, yh, c = me // 4, lax.rem(me // 2, 2), lax.rem(me, 2)
    x, yl = group // 2, lax.rem(group, 2)
    head = group * 2 + yh
    other_core = (z * 4 + yh * 2 + 1 - c, group)
    next_z = (lax.rem(z + 1, NZ) * 4 + yh * 2 + c, group)
    last_z = (lax.rem(z + NZ - 1, NZ) * 4 + yh * 2 + c, group)
    swap = (z * 4 + (1 - yh) * 2 + c, group)

    def plane_peer(dx, dl, dh):
        there = lax.rem(x + dx, 4) * 2 + lax.rem(yl + dl, 2)
        return (z * 4 + lax.rem(yh + dh, 2) * 2 + c, there)

    barrier = pltpu.get_barrier_semaphore()
    everyone = [other_core, next_z, last_z] + [plane_peer(*d) for d in PEERS]
    for peer in everyone:
        pl.semaphore_signal(barrier, inc=1, device_id=peer, device_id_type=MESH)

    here = pl.ds(pl.multiple_of(yh * 128, 128), 128)
    there = pl.ds(pl.multiple_of((1 - yh) * 128, 128), 128)
    columns = pl.ds(pl.multiple_of(group * 384, 384), 384)
    local = {
        KEYS: pltpu.make_async_copy(stale_keys.at[:, here], kbuf.at[me], loc_sem.at[0]),
        VALUES: pltpu.make_async_copy(stale_values.at[:, here], vbuf.at[me], loc_sem.at[1]),
        "hidden": pltpu.make_async_copy(hidden, hid.at[yh, group], loc_sem.at[2]),
        "shift": pltpu.make_async_copy(shift, shift_row, loc_sem.at[3]),
        "scale": pltpu.make_async_copy(scale, scale_row, loc_sem.at[4]),
        "text_keys": pltpu.make_async_copy(text_keys.at[:, here], text.at[0], loc_sem.at[5]),
        "text_values": pltpu.make_async_copy(text_values.at[:, here], text.at[1], loc_sem.at[6]),
        "query_gain": pltpu.make_async_copy(query_gain, gains.at[0], loc_sem.at[7]),
        "key_gain": pltpu.make_async_copy(key_gain, gains.at[1], loc_sem.at[8]),
        "gate": pltpu.make_async_copy(gate, gate_row, loc_sem.at[9]),
        "out_weight": pltpu.make_async_copy(
            out_weight.at[:, columns], wo.at[group], loc_sem.at[10]
        ),
    }
    for part in range(3):
        local[part] = pltpu.make_async_copy(
            weight.at[part, :, here],
            wbuf.at[me, :, pl.ds(part * 128, 128)],
            loc_sem.at[11 + part],
        )
    for name in (0, 1, 2, KEYS, VALUES):
        local[name].start()
    for name, copy in local.items():
        if name not in (0, 1, 2, KEYS, VALUES):
            copy.start()

    pl.semaphore_wait(barrier, len(everyone))

    def chunk(kind, stream, offset, core):
        side = yh if stream == 0 else 1 - yh
        index = lax.rem(z + offset + NZ, NZ) * 4 + side * 2 + core
        return {WEIGHTS: wbuf, KEYS: kbuf, VALUES: vbuf}[kind].at[index]

    def ring(kind, stream, way, step):
        ref = chunk(kind, stream, (1 - step) if way == 0 else (step - 1), c)
        at = (KINDS.index(kind) * 2 + stream) * 2 + way
        return COPY(
            ref, ref, ring_send.at[at, step], ring_recv.at[at, step],
            device_id=next_z if way == 0 else last_z, device_id_type=MESH,
        )

    def ring_arrival(kind, stream, way, step):
        ref = chunk(kind, stream, -step if way == 0 else step, c)
        at = (KINDS.index(kind) * 2 + stream) * 2 + way
        return COPY(
            ref, ref, ring_send.at[at, step], ring_recv.at[at, step],
            device_id=next_z if way == 0 else last_z, device_id_type=MESH,
        )

    def sibling(kind, stream, offset, core):
        ref = chunk(kind, stream, offset, core)
        at, slot = KINDS.index(kind) * 2 + stream, lax.rem(offset + NZ, NZ)
        return COPY(
            ref, ref, sib_send.at[at, slot], sib_recv.at[at, slot],
            device_id=other_core, device_id_type=MESH,
        )

    def swap_copy(src, dst, at):
        return COPY(
            src, dst, swap_send.at[at], swap_recv.at[at], device_id=swap, device_id_type=MESH
        )

    partner = z * 4 + (1 - yh) * 2 + c
    swaps = [
        swap_copy(stale_keys.at[:, there], kbuf.at[me], 0),
        swap_copy(stale_values.at[:, there], vbuf.at[me], 1),
    ]
    swaps += [
        swap_copy(weight.at[part, :, there], wbuf.at[me, :, pl.ds(part * 128, 128)], 2 + part)
        for part in range(3)
    ]
    swap_arrivals = [
        swap_copy(kbuf.at[partner], kbuf.at[partner], 0),
        swap_copy(vbuf.at[partner], vbuf.at[partner], 1),
    ]
    for part in range(3):
        slot = wbuf.at[partner, :, pl.ds(part * 128, 128)]
        swap_arrivals.append(swap_copy(slot, slot, 2 + part))

    def hid_copy(at, dx, dl, dh):
        return COPY(
            hidden, hid.at[yh, group], hid_send.at[at], hid_recv.at[at],
            device_id=plane_peer(dx, dl, dh), device_id_type=MESH,
        )

    def source_group(dx, dl):
        return lax.rem(x + 4 - dx, 4) * 2 + lax.rem(yl + dl, 2)

    def hid_arrival(at, dx, dl, dh):
        slot = hid.at[lax.rem(yh + dh, 2), source_group(dx, dl)]
        return COPY(
            slot, slot, hid_send.at[at], hid_recv.at[at],
            device_id=plane_peer(dx, dl, dh), device_id_type=MESH,
        )

    half = pl.ds(pl.multiple_of(c * 128, 128), 128)
    other_half = pl.ds(pl.multiple_of((1 - c) * 128, 128), 128)

    def wo_copy(at, dx, dl):
        peer = plane_peer(dx, dl, 0)
        src = out_weight.at[half, pl.ds(pl.multiple_of(peer[1] * 384, 384), 384)]
        return COPY(
            src, wo.at[group, half], wo_send.at[at], wo_recv.at[at],
            device_id=peer, device_id_type=MESH,
        )

    def wo_arrival(at, dx, dl):
        slot = wo.at[source_group(dx, dl), half]
        return COPY(
            slot, slot, wo_send.at[at], wo_recv.at[at],
            device_id=plane_peer(dx, dl, 0), device_id_type=MESH,
        )

    def wo_share(at, dx, dl, rows):
        slot = wo.at[source_group(dx, dl), rows]
        return COPY(
            slot, slot, wos_send.at[at], wos_recv.at[at],
            device_id=other_core, device_id_type=MESH,
        )

    def forward(kind, stream, step):
        if step == 0:
            if stream == 1:
                at = KINDS.index(kind)
                for copy in swap_arrivals[2:] if at == 0 else swap_arrivals[at - 1 : at]:
                    copy.wait_recv()
            else:
                for name in (0, 1, 2) if kind == WEIGHTS else (kind,):
                    local[name].wait()
            ring(kind, stream, 0, 1).start()
            ring(kind, stream, 1, 1).start()
            sibling(kind, stream, 0, c).start()
            return
        for way in (0, 1):
            if step < 8 or stream == way:
                ring_arrival(kind, stream, way, step).wait_recv()
                if step < 7 or step == 7 and stream == way:
                    ring(kind, stream, way, step + 1).start()
                sibling(kind, stream, -step if way == 0 else step, c).start()

    def norm(part):
        side, begin = part // 2, part % 2 * 4

        @pl.loop(begin, begin + 4, unroll=2)
        def _(block):
            rows = pl.ds(pl.multiple_of(block * 16, 16), 16)
            states = jnp.concatenate([hid[side, g, rows, :] for g in range(8)], axis=1)
            states = states.astype(F32)
            center = jnp.mean(states, axis=-1, keepdims=True)
            states = states - center
            spread = jnp.mean(states * states, axis=-1, keepdims=True)
            normed = states * lax.rsqrt(spread + 1e-06)
            modulated = (1.0 + scale_row[...]) * normed + shift_row[...]
            there = pl.ds(pl.multiple_of(side * 128 + block * 16, 16), 16)
            mod[there, :] = modulated.astype(BF16)

    def arrive_hidden():
        for name in ("hidden", "shift", "scale"):
            local[name].wait()
        for at, d in enumerate(PEERS):
            hid_arrival(at, *d).wait_recv()
        for at, d in enumerate(OUT_PEERS):
            wo_copy(at, *d).start()

    def project():
        @pl.loop(0, NZ)
        def _(slot):
            sibling(WEIGHTS, 0, slot, 1 - c).wait_recv()
            sibling(WEIGHTS, 1, slot, 1 - c).wait_recv()

        proj[...] = jnp.dot(mod[...], wbuf[...].reshape(3072, 384), preferred_element_type=F32)
        for name in ("text_keys", "text_values", "query_gain", "key_gain"):
            local[name].wait()
        queries[...] = head_norm(proj[:, 0:128], gains[0])

    def head_norm(raw, gain):
        power = jnp.mean(raw * raw, axis=-1, keepdims=True)
        return (raw * lax.rsqrt(power + 1e-06) * gain).astype(BF16)


    def scores_of(rows, keys):
        return lax.dot_general(
            queries[rows, :], keys, (((1,), (1,)), ((), ())), preferred_element_type=F32
        )

    def lane_sums(exps):
        parts = [exps[:, i : i + 128] for i in range(0, exps.shape[1], 128)]
        return functools.reduce(lambda a, b: a + b, parts)

    def start_attend(rows, keys, values):
        scores = scores_of(rows, keys)
        top = jnp.max(scores, axis=-1, keepdims=True)
        exps = jnp.exp2((scores - top) * EXP_SCALE)
        peak[rows, :] = jnp.broadcast_to(top, (scores.shape[0], 128))
        total[rows, :] = lane_sums(exps)
        mixed[rows, :] = jnp.dot(exps.astype(BF16), values, preferred_element_type=F32)

    def attend(rows, keys, values):
        scores = scores_of(rows, keys)
        before = peak[rows, :]
        top = jnp.maximum(before, jnp.max(scores, axis=-1, keepdims=True))
        rescale = jnp.exp2((before - top) * EXP_SCALE)
        exps = jnp.exp2((scores - top[:, 0:1]) * EXP_SCALE)
        peak[rows, :] = top
        total[rows, :] = total[rows, :] * rescale + lane_sums(exps)
        mixed[rows, :] = mixed[rows, :] * rescale + jnp.dot(
            exps.astype(BF16), values, preferred_element_type=F32
        )

    every = pl.ds(0, 256)

    def siblings_of(offset):
        for kind in (KEYS, VALUES):
            for stream in (0, 1):
                sibling(kind, stream, offset, 1 - c).wait_recv()

    def attend_own():
        start_attend(every, text[0], text[1])
        siblings_of(0)
        for side in (0, 1):
            rows = pl.ds(side * 128, 128)
            own_keys[...] = kbuf[pl.ds(z * 4, 4)]
            own_values[...] = vbuf[pl.ds(z * 4, 4)]
            own_keys[side * 2 + c] = head_norm(proj[rows, 128:256], gains[1])
            own_values[side * 2 + c] = proj[rows, 256:384].astype(BF16)
            attend(rows, own_keys[...].reshape(512, 128), own_values[...].reshape(512, 128))

    def plane(buf, offset):
        return buf[pl.ds(lax.rem(z + offset, NZ) * 4, 4)].reshape(512, 128)

    def attend_pairs(first, count):
        @pl.loop(first, first + count)
        def _(distance):
            offsets = (distance, NZ - distance)
            for offset in offsets:
                siblings_of(offset)
            keys = jnp.concatenate([plane(kbuf, offset) for offset in offsets], axis=0)
            values = jnp.concatenate([plane(vbuf, offset) for offset in offsets], axis=0)
            attend(every, keys, values)

    def attend_last():
        siblings_of(8)
        attend(every, plane(kbuf, 8), plane(vbuf, 8))

    def share():
        for at, d in enumerate(OUT_PEERS):
            wo_arrival(at, *d).wait_recv()
            wo_share(at, *d, half).start()

    for copy in swaps[2:]:
        copy.start()
    forward(WEIGHTS, 0, 0)
    for copy in swaps[:2]:
        copy.start()
    forward(KEYS, 0, 0)
    forward(VALUES, 0, 0)

    hidden_due = list(enumerate(PEERS))
    for task, first, second in ORDER:
        if hidden_due:
            at, d = hidden_due.pop()
            hid_copy(at, *d).start()
        if task in KINDS:
            forward(task, first, second)
        elif task == "N":
            if first == 0:
                arrive_hidden()
            norm(first)
        elif task == "P":
            project()
        elif task == "O":
            attend_own()
        elif task == "S":
            share()
        elif task == "A":
            attend_pairs(first, second)
        else:
            attend_last()

    def attention(side):
        rows = pl.ds(side * 128, 128)
        sums = jnp.sum(total[rows, :], axis=-1, keepdims=True)
        return (mixed[rows, :] / sums).astype(BF16)

    def att_copy(at, dx, dl, dh):
        return COPY(
            mine.at[lax.rem(yh + dh, 2)], gathered.at[head], att_send.at[at], att_recv.at[at],
            device_id=plane_peer(dx, dl, dh), device_id_type=MESH,
        )

    def att_arrival(at, dx, dl, dh):
        slot = gathered.at[source_group(dx, dl) * 2 + lax.rem(yh + dh, 2)]
        return COPY(
            slot, slot, att_send.at[at], att_recv.at[at],
            device_id=plane_peer(dx, dl, dh), device_id_type=MESH,
        )

    def send_attention(dh):
        side = lax.rem(yh + dh, 2)
        mine[side] = attention(side)
        for at, d in reversed(list(enumerate(PEERS))):
            if d[2] == dh:
                att_copy(at, *d).start()

    send_attention(1)
    send_attention(0)
    gathered[head] = mine[yh]
    local["out_weight"].wait()
    local["gate"].wait()
    for at, d in enumerate(OUT_PEERS):
        wo_share(at, *d, other_half).wait_recv()
    for at, d in enumerate(PEERS):
        att_arrival(at, *d).wait_recv()
    summed = jnp.zeros((128, 384), F32)
    for g in range(8):
        left = jnp.concatenate([gathered[2 * g], gathered[2 * g + 1]], axis=1)
        summed += jnp.dot(left, wo[g], preferred_element_type=F32)
    out[...] = (summed * gate_row[...].reshape(1, 384)).astype(BF16)

    for copy in swaps:
        copy.wait_send()
    for at, d in enumerate(PEERS):
        hid_copy(at, *d).wait_send()
        att_copy(at, *d).wait_send()
    for at, d in enumerate(OUT_PEERS):
        wo_copy(at, *d).wait_send()
        wo_share(at, *d, half).wait_send()
    for kind in KINDS:
        for stream in (0, 1):
            for way in (0, 1):
                @pl.loop(1, 8)
                def _(step):
                    ring(kind, stream, way, step).wait_send()
            ring(kind, stream, stream, 8).wait_send()

            @pl.loop(0, NZ)
            def _(slot):
                sibling(kind, stream, slot, c).wait_send()


def per_device(
    hidden_states,
    shift_mod,
    scale_mod,
    gate_mod,
    qkv_weight,
    query_gain,
    key_gain,
    text_keys,
    text_values,
    stale_keys,
    stale_values,
    out_weight,
):
    dma = pltpu.SemaphoreType.DMA
    vmem = pl.BlockSpec(memory_space=pltpu.VMEM)
    hbm = pl.BlockSpec(memory_space=pltpu.HBM)
    n, m = len(PEERS), len(OUT_PEERS)
    return pl.pallas_call(
        kernel,
        name="joint_attention",
        out_shape=jax.ShapeDtypeStruct((128, 384), BF16),
        in_specs=[hbm] * 12,
        out_specs=vmem,
        scratch_shapes=[
            pltpu.VMEM((2, 8, 128, 384), BF16),
            pltpu.VMEM((256, 3072), BF16),
            pltpu.VMEM((64, 48, 384), BF16),
            pltpu.VMEM((64, 128, 128), BF16),
            pltpu.VMEM((64, 128, 128), BF16),
            pltpu.VMEM((1, 3072), F32),
            pltpu.VMEM((1, 3072), F32),
            pltpu.VMEM((384,), F32),
            pltpu.VMEM((2, 1, 128), F32),
            pltpu.VMEM((2, 512, 128), BF16),
            pltpu.VMEM((8, 256, 384), BF16),
            pltpu.VMEM((16, 128, 128), BF16),
            pltpu.VMEM((2, 128, 128), BF16),
            pltpu.VMEM((4, 128, 128), BF16),
            pltpu.VMEM((4, 128, 128), BF16),
            pltpu.VMEM((256, 384), F32),
            pltpu.VMEM((256, 128), BF16),
            pltpu.VMEM((256, 128), F32),
            pltpu.VMEM((256, 128), F32),
            pltpu.VMEM((256, 128), F32),
            dma((14,)),
            dma((5,)),
            dma((5,)),
            dma((12, 9)),
            dma((12, 9)),
            dma((6, NZ)),
            dma((6, NZ)),
            dma((n,)),
            dma((n,)),
            dma((m,)),
            dma((m,)),
            dma((m,)),
            dma((m,)),
            dma((n,)),
            dma((n,)),
        ],
        compiler_params=pltpu.CompilerParams(
            collective_id=0, has_side_effects=True, vmem_limit_bytes=60 * 1024 * 1024
        ),
        cost_estimate=pl.CostEstimate(
            flops=2_200_000_000, bytes_accessed=16_000_000, transcendentals=2_300_000
        ),
    )(
        hidden_states,
        shift_mod.reshape(1, -1),
        scale_mod.reshape(1, -1),
        gate_mod,
        qkv_weight.transpose(1, 0, 2),
        query_gain.reshape(1, -1),
        key_gain.reshape(1, -1),
        text_keys,
        text_values,
        stale_keys,
        stale_values,
        out_weight,
    )


def solution(mesh):
    placed = (
        P("patch", "head"),
        P(),
        P(),
        P("head"),
        P("patch", None, "head"),
        P(),
        P(),
        P(None, "head"),
        P(None, "head"),
        P("patch", "head"),
        P("patch", "head"),
        P("head", None),
    )
    return jax.shard_map(
        per_device, mesh=mesh, in_specs=placed, out_specs=P("patch", "head"), check_vma=False
    )
```

time: 111 us -> 77.6 us (0.70); the launches traced: 109 us -> 76.7 us
  Pallas kernels: 97.9 us -> 75.1 us
  local copies, waits for them, and re-layouts: 10.9 us -> 1.54 us
    pallas_call x1, Pallas kernels: 97.9 us -> 75.1 us  [per_device(): pl.pallas_call(kernel, name='joint_attention', out_shape=jax.ShapeDtypeSt...]
    unnamed x21 -> x1, local copies, waits for them, and re-layouts: 9.24 us -> 1.54 us
    reshape x4 -> x0, local copies, waits for them, and re-layouts: 1.71 us -> none  [the longest x3 1.03 us: per_device(): qkv_weight.reshape(48, 3, 2, 128).transpose(2, 0, 1, 3).reshape(2, 48, 384)]
where the time goes in v2:
time: 77.6 us; the launch traced here: 76.7 us
  Pallas kernels  75.1 us (97%)
  local copies, waits for them, and re-layouts  1.54 us (2%)
    pallas_call x1, Pallas kernels, per_device(): pl.pallas_call(kernel, name='joint_attention', out_shape=jax.ShapeDtypeSt...  75.1 us

profile of v2, /device:TPU:1, one launch (start us, length us, event | category | flops | bytes accessed | tf_op | source)
XLA Modules:
  0.0 76.7 jit_solution(16604027182395584626)
XLA Ops:
  0.0 75.1 %joint_attention.1 = bf16[128,384]{1,0:T(8,128)(2,1)} custom-call(bf16[128,384]{1,0:T(8,128)(2,1)} %hidden.1, f32[1,3072]{1,0:T(1,128)} %bitcast.6, f32[1,3072]{1,0:T(1,128)} %bitcast.7, f32[384]{0:T(512)} %gate.1, bf16[3,48,256]{2,1,0:T(8,128)(2,1)} %bitcast.5, f32[1,128]{1,0:T(1,128)} %bitcast.8, f32[1,128]{1,0:T(1,128)} %bitcast.9, ...), custom_call_target="tpu_custom_call" | custom-call | flops 2200000000 | bytes 16000000 | tf_op jit(solution)/shard_map/joint_attention/pallas_call | solution.py:466
  75.1 1.5 %copy.14 = bf16[128,384]{1,0:T(8,128)(2,1)} copy(bf16[128,384]{1,0:T(8,128)(2,1)} %joint_attention.1) | data formatting | bytes 196608

commit v3 on v2

--- a/solution.py
+++ b/solution.py
@@ -12,13 +12,13 @@
 MESH = pl.DeviceIdType.MESH
 ORDER = (
     ("W", 0, 1), ("K", 0, 1), ("W", 1, 0), ("V", 0, 1), ("K", 1, 0), ("W", 0, 2), ("V", 1, 0), ("W", 1, 1),
-    ("K", 0, 2), ("W", 0, 3), ("V", 0, 2), ("W", 1, 2), ("K", 1, 1), ("V", 1, 1), ("W", 0, 4), ("K", 0, 3),
-    ("W", 1, 3), ("V", 0, 3), ("K", 1, 2), ("W", 0, 5), ("V", 1, 2), ("W", 1, 4), ("K", 0, 4), ("V", 0, 4),
-    ("W", 0, 6), ("K", 1, 3), ("W", 1, 5), ("V", 1, 3), ("N", 0, 0), ("K", 0, 5), ("N", 1, 0), ("W", 0, 7),
-    ("N", 2, 0), ("V", 0, 5), ("N", 3, 0), ("K", 1, 4), ("W", 1, 6), ("V", 1, 4), ("W", 0, 8), ("K", 0, 6),
-    ("V", 0, 6), ("K", 1, 5), ("W", 1, 7), ("V", 1, 5), ("K", 0, 7), ("V", 0, 7), ("K", 1, 6), ("W", 1, 8),
-    ("V", 1, 6), ("K", 0, 8), ("P", 0, 0), ("V", 0, 8), ("K", 1, 7), ("O", 0, 0), ("S", 0, 0), ("V", 1, 7),
-    ("A", 1, 2), ("K", 1, 8), ("A", 3, 1), ("V", 1, 8), ("A", 4, 4), ("L", 0, 0),
+    ("K", 0, 2), ("W", 0, 3), ("K", 1, 1), ("W", 1, 2), ("V", 1, 1), ("V", 0, 2), ("W", 0, 4), ("K", 1, 2),
+    ("W", 1, 3), ("V", 1, 2), ("K", 0, 3), ("W", 0, 5), ("V", 0, 3), ("W", 1, 4), ("K", 1, 3), ("V", 1, 3),
+    ("W", 0, 6), ("K", 0, 4), ("W", 1, 5), ("V", 0, 4), ("K", 1, 4), ("N", 0, 0), ("W", 0, 7), ("N", 1, 0),
+    ("V", 1, 4), ("N", 2, 0), ("W", 1, 6), ("N", 3, 0), ("Q", 0, 0), ("K", 0, 5), ("V", 0, 5), ("W", 0, 8), ("K", 1, 5),
+    ("V", 1, 5), ("W", 1, 7), ("K", 0, 6), ("V", 0, 6), ("K", 1, 6), ("V", 1, 6), ("W", 1, 8), ("K", 0, 7),
+    ("P", 0, 0), ("V", 0, 7), ("K", 1, 7), ("V", 1, 7), ("O", 0, 0), ("K", 0, 8), ("A", 1, 2), ("S", 0, 0),
+    ("V", 0, 8), ("K", 1, 8), ("V", 1, 8), ("A", 3, 4), ("L", 0, 0),
 )
 WEIGHTS, KEYS, VALUES = "WKV"
 KINDS = (WEIGHTS, KEYS, VALUES)
@@ -48,9 +48,10 @@
     out,
     hid,
     mod,
+    stage,
+    stage_kv,
     wbuf,
-    kbuf,
-    vbuf,
+    kv,
     shift_row,
     scale_row,
     gate_row,
@@ -97,7 +98,7 @@
         return (z * 4 + lax.rem(yh + dh, 2) * 2 + c, there)
 
     barrier = pltpu.get_barrier_semaphore()
-    everyone = [other_core, next_z, last_z] + [plane_peer(*d) for d in PEERS]
+    everyone = [plane_peer(*d) for d in PEERS[::-1]] + [next_z, last_z, other_core]
     for peer in everyone:
         pl.semaphore_signal(barrier, inc=1, device_id=peer, device_id_type=MESH)
 
@@ -105,8 +106,8 @@
     there = pl.ds(pl.multiple_of((1 - yh) * 128, 128), 128)
     columns = pl.ds(pl.multiple_of(group * 384, 384), 384)
     local = {
-        KEYS: pltpu.make_async_copy(stale_keys.at[:, here], kbuf.at[me], loc_sem.at[0]),
-        VALUES: pltpu.make_async_copy(stale_values.at[:, here], vbuf.at[me], loc_sem.at[1]),
+        KEYS: pltpu.make_async_copy(stale_keys.at[:, here], kv.at[me, 0], loc_sem.at[0]),
+        VALUES: pltpu.make_async_copy(stale_values.at[:, here], kv.at[me, 1], loc_sem.at[1]),
         "hidden": pltpu.make_async_copy(hidden, hid.at[yh, group], loc_sem.at[2]),
         "shift": pltpu.make_async_copy(shift, shift_row, loc_sem.at[3]),
         "scale": pltpu.make_async_copy(scale, scale_row, loc_sem.at[4]),
@@ -119,24 +120,27 @@
             out_weight.at[:, columns], wo.at[group], loc_sem.at[10]
         ),
     }
-    for part in range(3):
-        local[part] = pltpu.make_async_copy(
-            weight.at[part, :, here],
-            wbuf.at[me, :, pl.ds(part * 128, 128)],
-            loc_sem.at[11 + part],
-        )
-    for name in (0, 1, 2, KEYS, VALUES):
+    local[WEIGHTS] = pltpu.make_async_copy(weight.at[:, :, here], wbuf.at[me], loc_sem.at[11])
+    staged = {
+        WEIGHTS: pltpu.make_async_copy(weight.at[:, :, there], stage, loc_sem.at[12]),
+        KEYS: pltpu.make_async_copy(stale_keys.at[:, there], stage_kv.at[0], loc_sem.at[13]),
+        VALUES: pltpu.make_async_copy(stale_values.at[:, there], stage_kv.at[1], loc_sem.at[14]),
+    }
+    for name in KINDS:
         local[name].start()
+        staged[name].start()
     for name, copy in local.items():
-        if name not in (0, 1, 2, KEYS, VALUES):
+        if name not in KINDS:
             copy.start()
 
+    for copy in staged.values():
+        copy.wait()
     pl.semaphore_wait(barrier, len(everyone))
 
     def chunk(kind, stream, offset, core):
         side = yh if stream == 0 else 1 - yh
         index = lax.rem(z + offset + NZ, NZ) * 4 + side * 2 + core
-        return {WEIGHTS: wbuf, KEYS: kbuf, VALUES: vbuf}[kind].at[index]
+        return wbuf.at[index] if kind == WEIGHTS else kv.at[index, KINDS.index(kind) - 1]
 
     def ring(kind, stream, way, step):
         ref = chunk(kind, stream, (1 - step) if way == 0 else (step - 1), c)
@@ -155,8 +159,11 @@
         )
 
     def sibling(kind, stream, offset, core):
-        ref = chunk(kind, stream, offset, core)
-        at, slot = KINDS.index(kind) * 2 + stream, lax.rem(offset + NZ, NZ)
+        side = yh if stream == 0 else 1 - yh
+        slot = lax.rem(offset + NZ, NZ)
+        index = lax.rem(z + slot, NZ) * 4 + side * 2 + core
+        ref = wbuf.at[index] if kind == WEIGHTS else kv.at[index]
+        at = (kind == VALUES) * 2 + stream
         return COPY(
             ref, ref, sib_send.at[at, slot], sib_recv.at[at, slot],
             device_id=other_core, device_id_type=MESH,
@@ -169,20 +176,15 @@
 
     partner = z * 4 + (1 - yh) * 2 + c
     swaps = [
-        swap_copy(stale_keys.at[:, there], kbuf.at[me], 0),
-        swap_copy(stale_values.at[:, there], vbuf.at[me], 1),
-    ]
-    swaps += [
-        swap_copy(weight.at[part, :, there], wbuf.at[me, :, pl.ds(part * 128, 128)], 2 + part)
-        for part in range(3)
+        swap_copy(stage, wbuf.at[me], 0),
+        swap_copy(stage_kv.at[0], kv.at[me, 0], 1),
+        swap_copy(stage_kv.at[1], kv.at[me, 1], 2),
     ]
     swap_arrivals = [
-        swap_copy(kbuf.at[partner], kbuf.at[partner], 0),
-        swap_copy(vbuf.at[partner], vbuf.at[partner], 1),
+        swap_copy(wbuf.at[partner], wbuf.at[partner], 0),
+        swap_copy(kv.at[partner, 0], kv.at[partner, 0], 1),
+        swap_copy(kv.at[partner, 1], kv.at[partner, 1], 2),
     ]
-    for part in range(3):
-        slot = wbuf.at[partner, :, pl.ds(part * 128, 128)]
-        swap_arrivals.append(swap_copy(slot, slot, 2 + part))
 
     def hid_copy(at, dx, dl, dh):
         return COPY(
@@ -226,24 +228,23 @@
         )
 
     def forward(kind, stream, step):
+        if kind == WEIGHTS and step > 0:
+            for offset in {1 - step, step - 1}:
+                sibling(kind, stream, offset, 1 - c).wait_recv()
         if step == 0:
-            if stream == 1:
-                at = KINDS.index(kind)
-                for copy in swap_arrivals[2:] if at == 0 else swap_arrivals[at - 1 : at]:
-                    copy.wait_recv()
-            else:
-                for name in (0, 1, 2) if kind == WEIGHTS else (kind,):
-                    local[name].wait()
+            (swap_arrivals[KINDS.index(kind)].wait_recv if stream else local[kind].wait)()
             ring(kind, stream, 0, 1).start()
             ring(kind, stream, 1, 1).start()
-            sibling(kind, stream, 0, c).start()
+            if kind != KEYS:
+                sibling(kind, stream, 0, c).start()
             return
-        for way in (0, 1):
-            if step < 8 or stream == way:
-                ring_arrival(kind, stream, way, step).wait_recv()
-                if step < 7 or step == 7 and stream == way:
-                    ring(kind, stream, way, step + 1).start()
-                sibling(kind, stream, -step if way == 0 else step, c).start()
+        ways = [way for way in (0, 1) if step < 8 or stream == way]
+        for way in ways:
+            ring_arrival(kind, stream, way, step).wait_recv()
+            if step < 7 or step == 7 and stream == way:
+                ring(kind, stream, way, step + 1).start()
+        for way in ways if kind != KEYS else ():
+            sibling(kind, stream, -step if way == 0 else step, c).start()
 
     def norm(part):
         side, begin = part // 2, part % 2 * 4
@@ -269,13 +270,18 @@
         for at, d in enumerate(OUT_PEERS):
             wo_copy(at, *d).start()
 
-    def project():
-        @pl.loop(0, NZ)
-        def _(slot):
-            sibling(WEIGHTS, 0, slot, 1 - c).wait_recv()
-            sibling(WEIGHTS, 1, slot, 1 - c).wait_recv()
-
-        proj[...] = jnp.dot(mod[...], wbuf[...].reshape(3072, 384), preferred_element_type=F32)
+    def project(pairs):
+        for pair in pairs:
+            at = lax.rem(z // 2 + pair + 8, 8)
+            rows = [wbuf[pl.ds(at * 8, 8), part].reshape(384, 128) for part in range(3)]
+            features = mod[:, pl.ds(pl.multiple_of(at * 384, 384), 384)]
+            term = jnp.dot(features, jnp.concatenate(rows, axis=1), preferred_element_type=F32)
+            proj[...] = term if pair == 0 else proj[...] + term
+
+    def finish_projection():
+        for stream in (0, 1):
+            sibling(WEIGHTS, stream, 8, 1 - c).wait_recv()
+        project((-3, 3, 4))
         for name in ("text_keys", "text_values", "query_gain", "key_gain"):
             local[name].wait()
         queries[...] = head_norm(proj[:, 0:128], gains[0])
@@ -317,48 +323,48 @@
     every = pl.ds(0, 256)
 
     def siblings_of(offset):
-        for kind in (KEYS, VALUES):
-            for stream in (0, 1):
-                sibling(kind, stream, offset, 1 - c).wait_recv()
+        for stream in (0, 1):
+            sibling(VALUES, stream, offset, 1 - c).wait_recv()
 
     def attend_own():
         start_attend(every, text[0], text[1])
         siblings_of(0)
         for side in (0, 1):
             rows = pl.ds(side * 128, 128)
-            own_keys[...] = kbuf[pl.ds(z * 4, 4)]
-            own_values[...] = vbuf[pl.ds(z * 4, 4)]
+            own_keys[...] = kv[pl.ds(z * 4, 4), 0]
+            own_values[...] = kv[pl.ds(z * 4, 4), 1]
             own_keys[side * 2 + c] = head_norm(proj[rows, 128:256], gains[1])
             own_values[side * 2 + c] = proj[rows, 256:384].astype(BF16)
             attend(rows, own_keys[...].reshape(512, 128), own_values[...].reshape(512, 128))
 
-    def plane(buf, offset):
-        return buf[pl.ds(lax.rem(z + offset, NZ) * 4, 4)].reshape(512, 128)
+    def plane(which, offset):
+        return kv[pl.ds(lax.rem(z + offset, NZ) * 4, 4), which].reshape(512, 128)
+
+    def attend_planes(offsets):
+        for offset in offsets:
+            siblings_of(offset)
+        keys = jnp.concatenate([plane(0, offset) for offset in offsets], axis=0)
+        values = jnp.concatenate([plane(1, offset) for offset in offsets], axis=0)
+        attend(every, keys, values)
 
     def attend_pairs(first, count):
-        @pl.loop(first, first + count)
-        def _(distance):
-            offsets = (distance, NZ - distance)
-            for offset in offsets:
-                siblings_of(offset)
-            keys = jnp.concatenate([plane(kbuf, offset) for offset in offsets], axis=0)
-            values = jnp.concatenate([plane(vbuf, offset) for offset in offsets], axis=0)
-            attend(every, keys, values)
+        @pl.loop(0, count // 2)
+        def _(i):
+            near = first + 2 * i
+            attend_planes((near, NZ - near, near + 1, NZ - 1 - near))
 
     def attend_last():
-        siblings_of(8)
-        attend(every, plane(kbuf, 8), plane(vbuf, 8))
+        attend_planes((7, NZ - 7, 8))
 
     def share():
         for at, d in enumerate(OUT_PEERS):
             wo_arrival(at, *d).wait_recv()
             wo_share(at, *d, half).start()
 
-    for copy in swaps[2:]:
-        copy.start()
+    swaps[0].start()
     forward(WEIGHTS, 0, 0)
-    for copy in swaps[:2]:
-        copy.start()
+    swaps[1].start()
+    swaps[2].start()
     forward(KEYS, 0, 0)
     forward(VALUES, 0, 0)
 
@@ -373,8 +379,10 @@
             if first == 0:
                 arrive_hidden()
             norm(first)
+        elif task == "Q":
+            project((0, -1, 1, -2, 2))
         elif task == "P":
-            project()
+            finish_projection()
         elif task == "O":
             attend_own()
         elif task == "S":
@@ -411,6 +419,28 @@
 
     send_attention(1)
     send_attention(0)
+
+    for copy in swaps:
+        copy.wait_send()
+    for at, d in enumerate(PEERS):
+        hid_copy(at, *d).wait_send()
+    for at, d in enumerate(OUT_PEERS):
+        wo_copy(at, *d).wait_send()
+        wo_share(at, *d, half).wait_send()
+    for kind in KINDS:
+        for stream in (0, 1):
+            for way in (0, 1):
+
+                @pl.loop(1, 8)
+                def _(step):
+                    ring(kind, stream, way, step).wait_send()
+
+            ring(kind, stream, stream, 8).wait_send()
+
+            @pl.loop(0, NZ if kind != KEYS else 0)
+            def _(slot):
+                sibling(kind, stream, slot, c).wait_send()
+
     gathered[head] = mine[yh]
     local["out_weight"].wait()
     local["gate"].wait()
@@ -424,25 +454,8 @@
         summed += jnp.dot(left, wo[g], preferred_element_type=F32)
     out[...] = (summed * gate_row[...].reshape(1, 384)).astype(BF16)
 
-    for copy in swaps:
-        copy.wait_send()
     for at, d in enumerate(PEERS):
-        hid_copy(at, *d).wait_send()
         att_copy(at, *d).wait_send()
-    for at, d in enumerate(OUT_PEERS):
-        wo_copy(at, *d).wait_send()
-        wo_share(at, *d, half).wait_send()
-    for kind in KINDS:
-        for stream in (0, 1):
-            for way in (0, 1):
-                @pl.loop(1, 8)
-                def _(step):
-                    ring(kind, stream, way, step).wait_send()
-            ring(kind, stream, stream, 8).wait_send()
-
-            @pl.loop(0, NZ)
-            def _(slot):
-                sibling(kind, stream, slot, c).wait_send()
 
 
 def per_device(
@@ -472,9 +485,10 @@
         scratch_shapes=[
             pltpu.VMEM((2, 8, 128, 384), BF16),
             pltpu.VMEM((256, 3072), BF16),
-            pltpu.VMEM((64, 48, 384), BF16),
-            pltpu.VMEM((64, 128, 128), BF16),
-            pltpu.VMEM((64, 128, 128), BF16),
+            pltpu.VMEM((3, 48, 128), BF16),
+            pltpu.VMEM((2, 128, 128), BF16),
+            pltpu.VMEM((64, 3, 48, 128), BF16),
+            pltpu.VMEM((64, 2, 128, 128), BF16),
             pltpu.VMEM((1, 3072), F32),
             pltpu.VMEM((1, 3072), F32),
             pltpu.VMEM((384,), F32),
@@ -490,13 +504,13 @@
             pltpu.VMEM((256, 128), F32),
             pltpu.VMEM((256, 128), F32),
             pltpu.VMEM((256, 128), F32),
-            dma((14,)),
+            dma((15,)),
             dma((5,)),
             dma((5,)),
             dma((12, 9)),
             dma((12, 9)),
-            dma((6, NZ)),
-            dma((6, NZ)),
+            dma((4, NZ)),
+            dma((4, NZ)),
             dma((n,)),
             dma((n,)),
             dma((m,)),

time: 77.6 us -> 72.9 us (0.939)
  Pallas kernels: 75.1 us -> 71.2 us
    pallas_call x1, Pallas kernels: 75.1 us -> 71.2 us  [per_device(): pl.pallas_call(kernel, name='joint_attention', out_shape=jax.ShapeDtypeSt...]
where the time goes in v3:
time: 72.9 us; the launch traced here: 72.7 us
  Pallas kernels  71.2 us (98%)
  local copies, waits for them, and re-layouts  1.54 us (2%)
    pallas_call x1, Pallas kernels, per_device(): pl.pallas_call(kernel, name='joint_attention', out_shape=jax.ShapeDtypeSt...  71.2 us
    unnamed x1, local copies, waits for them, and re-layouts  1.54 us

profile of v3, /device:TPU:1, one launch (start us, length us, event | category | flops | bytes accessed | tf_op | source)
XLA Modules:
  0.0 72.7 jit_solution(5444984499272736518)
XLA Ops:
  0.0 71.2 %joint_attention.1 = bf16[128,384]{1,0:T(8,128)(2,1)} custom-call(bf16[128,384]{1,0:T(8,128)(2,1)} %hidden.1, f32[1,3072]{1,0:T(1,128)} %bitcast.6, f32[1,3072]{1,0:T(1,128)} %bitcast.7, f32[384]{0:T(512)} %gate.1, bf16[3,48,256]{2,1,0:T(8,128)(2,1)} %bitcast.5, f32[1,128]{1,0:T(1,128)} %bitcast.8, f32[1,128]{1,0:T(1,128)} %bitcast.9, ...), custom_call_target="tpu_custom_call" | custom-call | flops 2200000000 | bytes 16000000 | tf_op jit(solution)/shard_map/joint_attention/pallas_call | solution.py:479
  71.2 1.5 %copy.14 = bf16[128,384]{1,0:T(8,128)(2,1)} copy(bf16[128,384]{1,0:T(8,128)(2,1)} %joint_attention.1) | data formatting | bytes 196608

commit v4 on v3

--- a/solution.py
+++ b/solution.py
@@ -12,13 +12,13 @@
 MESH = pl.DeviceIdType.MESH
 ORDER = (
     ("W", 0, 1), ("K", 0, 1), ("W", 1, 0), ("V", 0, 1), ("K", 1, 0), ("W", 0, 2), ("V", 1, 0), ("W", 1, 1),
-    ("K", 0, 2), ("W", 0, 3), ("K", 1, 1), ("W", 1, 2), ("V", 1, 1), ("V", 0, 2), ("W", 0, 4), ("K", 1, 2),
+    ("K", 0, 2), ("W", 0, 3), ("K", 1, 1), ("V", 1, 1), ("W", 1, 2), ("V", 0, 2), ("W", 0, 4), ("K", 1, 2),
     ("W", 1, 3), ("V", 1, 2), ("K", 0, 3), ("W", 0, 5), ("V", 0, 3), ("W", 1, 4), ("K", 1, 3), ("V", 1, 3),
-    ("W", 0, 6), ("K", 0, 4), ("W", 1, 5), ("V", 0, 4), ("K", 1, 4), ("N", 0, 0), ("W", 0, 7), ("N", 1, 0),
-    ("V", 1, 4), ("N", 2, 0), ("W", 1, 6), ("N", 3, 0), ("Q", 0, 0), ("K", 0, 5), ("V", 0, 5), ("W", 0, 8), ("K", 1, 5),
-    ("V", 1, 5), ("W", 1, 7), ("K", 0, 6), ("V", 0, 6), ("K", 1, 6), ("V", 1, 6), ("W", 1, 8), ("K", 0, 7),
-    ("P", 0, 0), ("V", 0, 7), ("K", 1, 7), ("V", 1, 7), ("O", 0, 0), ("K", 0, 8), ("A", 1, 2), ("S", 0, 0),
-    ("V", 0, 8), ("K", 1, 8), ("V", 1, 8), ("A", 3, 4), ("L", 0, 0),
+    ("W", 0, 6), ("K", 0, 4), ("W", 1, 5), ("V", 0, 4), ("K", 1, 4), ("W", 0, 7), ("N", 0, 0), ("V", 1, 4),
+    ("N", 1, 0), ("K", 0, 5), ("N", 2, 0), ("W", 1, 6), ("N", 3, 0), ("Q", 0, 0), ("V", 0, 5), ("W", 0, 8),
+    ("K", 1, 5), ("V", 1, 5), ("K", 0, 6), ("W", 1, 7), ("V", 0, 6), ("K", 1, 6), ("V", 1, 6), ("K", 0, 7),
+    ("W", 1, 8), ("V", 0, 7), ("P", 0, 0), ("K", 1, 7), ("V", 1, 7), ("O", 0, 0), ("K", 0, 8), ("A", 1, 2),
+    ("S", 0, 0), ("V", 0, 8), ("K", 1, 8), ("V", 1, 8), ("A", 3, 4), ("L", 0, 0),
 )
 WEIGHTS, KEYS, VALUES = "WKV"
 KINDS = (WEIGHTS, KEYS, VALUES)

time: 72.9 us -> 72.1 us (0.989)
  Pallas kernels: 71.2 us -> 70.4 us
    pallas_call x1, Pallas kernels: 71.2 us -> 70.4 us  [per_device(): pl.pallas_call(kernel, name='joint_attention', out_shape=jax.ShapeDtypeSt...]
where the time goes in v4:
time: 72.1 us; the launch traced here: 72 us
  Pallas kernels  70.4 us (98%)
  local copies, waits for them, and re-layouts  1.54 us (2%)
    pallas_call x1, Pallas kernels, per_device(): pl.pallas_call(kernel, name='joint_attention', out_shape=jax.ShapeDtypeSt...  70.4 us
    unnamed x1, local copies, waits for them, and re-layouts  1.54 us

profile of v4, /device:TPU:1, one launch (start us, length us, event | category | flops | bytes accessed | tf_op | source)
XLA Modules:
  0.0 72.0 jit_solution(17091126874851938292)
XLA Ops:
  0.0 70.4 %joint_attention.1 = bf16[128,384]{1,0:T(8,128)(2,1)} custom-call(bf16[128,384]{1,0:T(8,128)(2,1)} %hidden.1, f32[1,3072]{1,0:T(1,128)} %bitcast.6, f32[1,3072]{1,0:T(1,128)} %bitcast.7, f32[384]{0:T(512)} %gate.1, bf16[3,48,256]{2,1,0:T(8,128)(2,1)} %bitcast.5, f32[1,128]{1,0:T(1,128)} %bitcast.8, f32[1,128]{1,0:T(1,128)} %bitcast.9, ...), custom_call_target="tpu_custom_call" | custom-call | flops 2200000000 | bytes 16000000 | tf_op jit(solution)/shard_map/joint_attention/pallas_call | solution.py:479
  70.4 1.5 %copy.14 = bf16[128,384]{1,0:T(8,128)(2,1)} copy(bf16[128,384]{1,0:T(8,128)(2,1)} %joint_attention.1) | data formatting | bytes 196608

commit v5 on v4

--- a/solution.py
+++ b/solution.py
@@ -446,10 +446,12 @@
     local["gate"].wait()
     for at, d in enumerate(OUT_PEERS):
         wo_share(at, *d, other_half).wait_recv()
-    for at, d in enumerate(PEERS):
-        att_arrival(at, *d).wait_recv()
     summed = jnp.zeros((128, 384), F32)
-    for g in range(8):
+    for dx, dl in ((0, 0), (1, 0), (3, 0), (0, 1), (1, 1), (3, 1), (2, 0), (2, 1)):
+        for dh in (0, 1):
+            if (dx, dl, dh) in PEERS:
+                att_arrival(PEERS.index((dx, dl, dh)), dx, dl, dh).wait_recv()
+        g = source_group(dx, dl)
         left = jnp.concatenate([gathered[2 * g], gathered[2 * g + 1]], axis=1)
         summed += jnp.dot(left, wo[g], preferred_element_type=F32)
     out[...] = (summed * gate_row[...].reshape(1, 384)).astype(BF16)

time: 72.1 us -> 72.6 us (level)
  no operation moved by 1% of the time
where the time goes in v5:
time: 72.6 us; the launch traced here: 72.4 us
  Pallas kernels  70.9 us (98%)
  local copies, waits for them, and re-layouts  1.54 us (2%)
    pallas_call x1, Pallas kernels, per_device(): pl.pallas_call(kernel, name='joint_attention', out_shape=jax.ShapeDtypeSt...  70.9 us
    unnamed x1, local copies, waits for them, and re-layouts  1.54 us

profile of v5, /device:TPU:1, one launch (start us, length us, event | category | flops | bytes accessed | tf_op | source)
XLA Modules:
  0.0 72.4 jit_solution(1193968654532429671)
XLA Ops:
  0.0 70.9 %joint_attention.1 = bf16[128,384]{1,0:T(8,128)(2,1)} custom-call(bf16[128,384]{1,0:T(8,128)(2,1)} %hidden.1, f32[1,3072]{1,0:T(1,128)} %bitcast.6, f32[1,3072]{1,0:T(1,128)} %bitcast.7, f32[384]{0:T(512)} %gate.1, bf16[3,48,256]{2,1,0:T(8,128)(2,1)} %bitcast.5, f32[1,128]{1,0:T(1,128)} %bitcast.8, f32[1,128]{1,0:T(1,128)} %bitcast.9, ...), custom_call_target="tpu_custom_call" | custom-call | flops 2200000000 | bytes 16000000 | tf_op jit(solution)/shard_map/joint_attention/pallas_call | solution.py:481
  70.9 1.5 %copy.14 = bf16[128,384]{1,0:T(8,128)(2,1)} copy(bf16[128,384]{1,0:T(8,128)(2,1)} %joint_attention.1) | data formatting | bytes 196608
